TPU v7x, 32 devices: a whole 2x2x4 slice. The times are simulated.
32 devices in a mesh: dom: 8 (over z, x), cls: 4 (over y, core).
Axes of the slice: x: 2, y: 2, z: 4, core: 2. Of those that a mesh axis runs over, the one named last changes fastest.
Arguments:
- particles: bfloat16 [256, 16384], P(('dom', 'cls')), may hold values from -6 to 6
- references: bfloat16 [64, 16384], P('cls'), may hold values from -0.046875 to 0.046875
- pose_weights: int32 [256, 24, 64], P(('dom', 'cls')), may hold values from 0 to 4
- class_mask: int32 [256, 64], P(('dom', 'cls')), may hold values 0 or 1
Outputs:
- class_scores: float32 [256, 64], P(('dom', 'cls'))
- class_sums: float32 [64, 16384], P('cls', 'dom')
All inputs are finite; a program needn't handle non-finite values. No bound on the sum of `class_mask` on one device may be relied on, other than what follows from the above.
Results may differ from a plain program's by a relative error of at most 0.0003.
Values may be sent and summed in bfloat16 or wider, within the bound.
No kernel may reach another device: no remote copies, remote signals or barrier semaphores. Data moves between devices by JAX's collectives and lax.ppermute only.
A program may use at most 128 MiB of HBM per device.

v0:
```python
import math
import jax
import jax.numpy as jnp
from jax import lax
from jax.sharding import PartitionSpec as P

CYCLES = 64
ANG = 256
ROT = 24


def turned(images, shift_by):
    shape_in = images.shape
    polar = images.reshape(shape_in[:-1] + (CYCLES, ANG))
    return jnp.roll(polar, shift_by, axis=-1).reshape(shape_in)


def on_device(particles, references, pose_weights, class_mask):
    n_rows = particles.shape[0]
    angle_step = ANG // ROT
    weights = pose_weights * class_mask[:, None, :]
    weights_f = weights.astype(jnp.float32)
    weights_b = weights.astype(jnp.bfloat16)
    rotated = jnp.stack([turned(particles, -r * angle_step) for r in range(ROT)], axis=0)
    rotated_rows = rotated.reshape(ROT * n_rows, rotated.shape[2])
    ref_piece = lax.all_gather(references, "cls", axis=0, tiled=True)
    width_now = ref_piece.shape[0]
    corr = jnp.dot(rotated_rows, ref_piece.T, preferred_element_type=jnp.float32)
    corr = corr.reshape(ROT, n_rows, width_now)
    weight_cols = weights_f
    scored = jnp.einsum("rnk,nrk->nk", corr, weight_cols) / ROT
    weight_cols = weights_b
    local_sums = lax.psum_scatter(
        jnp.einsum("nrk,rnl->kl", weight_cols, rotated, preferred_element_type=jnp.float32),
        "cls",
        scatter_dimension=0,
        tiled=True,
    )
    home_part = lax.psum_scatter(local_sums, "dom", scatter_dimension=1, tiled=True)
    particle_total = n_rows * lax.axis_size("dom") * lax.axis_size("cls")
    class_sums = home_part / math.sqrt(particle_total * ROT)
    return (scored, class_sums)


def solution(mesh):
    return jax.shard_map(
        on_device,
        mesh=mesh,
        in_specs=(
            P(("dom", "cls"), None),
            P("cls", None),
            P(("dom", "cls"), None, None),
            P(("dom", "cls"), None),
        ),
        out_specs=(P(("dom", "cls"), None), P("cls", "dom")),
        check_vma=False,
    )
```

profile of v0, /device:TPU:0, one launch (start us, length us, event | category | flops | bytes accessed | tf_op | source)
XLA Modules:
  0.0 300.9 jit_solution(10851470049415356779)
XLA Ops:
  20.6 1.8 slice.250
  24.0 1.8 slice.252
  49.3 1.8 stack_reshape.106
  53.8 1.8 stack_reshape.107
  58.3 1.7 stack_reshape.96
  62.8 1.8 stack_reshape.97
  67.3 1.8 stack_reshape.98
  71.8 1.8 stack_reshape.99
  75.4 1.7 stack_reshape.108
  79.0 1.7 stack_reshape.109
  82.6 1.8 stack_reshape.110
  86.2 1.8 stack_reshape.111
  89.7 1.7 stack_reshape.112
  93.3 1.7 stack_reshape.113
  96.9 1.8 stack_reshape.114
  100.5 1.8 stack_reshape.115
  104.1 1.7 stack_reshape.116
  110.3 1.8 stack_reshape.118
  113.3 34.4 %stack.3 = bf16[24,8,16384]{2,0,1:T(8,128)(2,1)} concatenate(bf16[1,8,16384]{2,0,1:T(2,128)(2,1)} %copy.98, bf16[1,8,16384]{2,0,1:T(2,128)(2,1)} %stack_reshape.96, bf16[1,8,16384]{2,0,1:T(2,128)(2,1)} %stack_reshape.97, bf16[1,8,16384]{2,0,1:T(2,128)(2,1)} %stack_reshape.98, bf16[1,8,16384]{2,0,1:T(2,128)(2,1)} %stack_reshape.99, bf16[1,8,16384]{2,0,1:T(2,128)(2,1)S(1)} %stack_reshape.100, ...), dimensions={0} | concatenate | bytes 12582912 | tf_op jit(solution)/shard_map/stack | solution.py:24
  147.7 6.2 %convolution_bitcast_fusion = f32[64,16384]{1,0:T(8,128)} fusion(bf16[24,8,16384]{2,0,1:T(8,128)(2,1)} %stack.3, s32[8,24,64]{2,1,0:T(8,128)S(1)} %copy-done.2, s32[8,64]{1,0:T(8,128)S(1)} %copy-done.1), kind=kOutput, calls=%fused_computation | convolution fusion | flops 402677760 | bytes 10536960 | tf_op jit(solution)/shard_map/nrk,rnl->kl/dot_general | solution.py:34
  154.7 46.6 %reduce-scatter.3.cloned.1.call-done = f32[16,16384]{1,0:T(8,128)} async-done(((f32[64,16384]{1,0:T(8,128)}), f32[16,16384]{1,0:T(8,128)}) %reduce-scatter.3.cloned.1.call-update) | async-done | bytes 1048592 | tf_op jit(solution)/shard_map/reduce_scatter | solution.py:33
  201.3 24.2 %all-gather.2.cloned.1.call-done = bf16[64,16384]{1,0:T(8,128)(2,1)} async-done(((bf16[16,16384]{1,0:T(8,128)(2,1)}), bf16[64,16384]{1,0:T(8,128)(2,1)}) %all-gather.2.cloned.1.call-update) | async-done | bytes 2097168 | tf_op jit(solution)/shard_map/all_gather | solution.py:26
  225.5 5.2 %fusion.8 = f32[8,64]{1,0:T(8,128)S(1)} fusion(bf16[24,8,16384]{2,0,1:T(8,128)(2,1)} %stack.3, bf16[64,16384]{1,0:T(8,128)(2,1)} %all-gather.2.cloned.1.call-done, s32[8,24,64]{2,1,0:T(8,128)S(1)} %copy-done.2, s32[8,64]{1,0:T(8,128)S(1)} %copy-done.1), kind=kOutput, calls=%fused_computation.5 | convolution fusion | flops 402701824 | bytes 8441856 | tf_op jit(solution)/shard_map/dot_general | solution.py:28
  231.3 61.4 %reduce-scatter.5.cloned.1.call-done = f32[16,2048]{1,0:T(8,128)} async-done(((f32[16,16384]{1,0:T(8,128)}), f32[16,2048]{1,0:T(8,128)}) %reduce-scatter.5.cloned.1.call-update) | async-done | bytes 131088 | tf_op jit(solution)/shard_map/reduce_scatter | solution.py:39
  (124 shorter events, 76.9 us)
Async XLA Ops:
  7.2 20.2 %copy-start = (bf16[8,16384]{1,0:T(8,128)(2,1)S(1)}, bf16[8,16384]{1,0:T(8,128)(2,1)}, u32[]{:S(2)}) copy-start(bf16[8,16384]{1,0:T(8,128)(2,1)} %param.4) | copy-start | bytes 786436
  7.2 194.1 %reduce-scatter.3.cloned.1.call-start = ((), (), s32[]{:S(2)}) async-start(), calls=%async_computation.3 | async-start | bytes 5242880 | tf_op jit(solution)/shard_map/reduce_scatter | solution.py:33
  113.3 34.4 %copy-start.1 = (s32[8,64]{1,0:T(8,128)S(1)}, s32[8,64]{1,0:T(8,128)}, u32[]{:S(2)}) copy-start(s32[8,64]{1,0:T(8,128)} %param.7) | copy-start | bytes 6148
  113.3 34.4 %copy-start.2 = (s32[8,24,64]{2,1,0:T(8,128)S(1)}, s32[8,24,64]{2,1,0:T(8,128)}, u32[]{:S(2)}) copy-start(s32[8,24,64]{2,1,0:T(8,128)} %param.6) | copy-start | bytes 147460
  153.9 71.6 %all-gather.2.cloned.1.call-start = ((), (), s32[]{:S(2)}) async-start(), calls=%async_computation.2 | async-start | bytes 2621440 | tf_op jit(solution)/shard_map/all_gather | solution.py:26
  154.6 138.1 %reduce-scatter.5.cloned.1.call-start = ((), (), s32[]{:S(2)}) async-start(), calls=%async_computation.4 | async-start | bytes 1179648 | tf_op jit(solution)/shard_map/reduce_scatter | solution.py:39
Sparse Core Ops, SparseCore 0:
  154.0 47.2 reduce-scatter.2
  202.9 22.5 all-gather.1
  229.3 63.4 reduce-scatter.4
where the time goes:
time: 306 us; the launch traced here: 301 us
  waiting for transfers between devices  133 us (43%)
  local copies, waits for them, and re-layouts  125 us (41%)
  other arithmetic  17.7 us (6%)
  between operations  14.2 us (5%)
  matrix products  11.4 us (4%)
    another operation x25, local copies, waits for them, and re-layouts, on_device(): jnp.stack([turned(particles, -r * angle_step) for r in range(ROT)], axis=0)  67.3 us
    reduce_scatter x1, waiting for transfers between devices, on_device(): lax.psum_scatter(local_sums, 'dom', scatter_dimension=1, tiled=True)  61.4 us
    reduce_scatter x1, waiting for transfers between devices, on_device(): lax.psum_scatter(jnp.einsum('nrk,rnl->kl', weight_cols, rotated, preferre...  46.6 us
    slice x35, local copies, waits for them, and re-layouts, turned(): return jnp.roll(polar, shift_by, axis=-1).reshape(shape_in)  33.7 us
    all_gather x1, waiting for transfers between devices, on_device(): ref_piece = lax.all_gather(references, 'cls', axis=0, tiled=True)  24.2 us
    unnamed x52, local copies, waits for them, and re-layouts  23.6 us
    concatenate x23, other arithmetic, turned(): return jnp.roll(polar, shift_by, axis=-1).reshape(shape_in)  15.5 us
    dot_general x1, matrix products, on_device(): jnp.einsum('nrk,rnl->kl', weight_cols, rotated, preferred_element_type=jn...  6.15 us
  transfers between devices with their start and end apart: 3, of which 3 were waited for; matrix products, arithmetic and copies ran while one was open for 2% of the time, Pallas kernels for 0%

commit v1 on v0

--- a/solution.py
+++ b/solution.py
@@ -23,7 +23,12 @@
     weights_b = weights.astype(jnp.bfloat16)
     rotated = jnp.stack([turned(particles, -r * angle_step) for r in range(ROT)], axis=0)
     rotated_rows = rotated.reshape(ROT * n_rows, rotated.shape[2])
-    ref_piece = lax.all_gather(references, "cls", axis=0, tiled=True)
+    ring = [references]
+    for hop in range(3):
+        ring.append(lax.ppermute(ring[-1], "cls", [(dev, (dev + 1) % 4) for dev in range(4)]))
+    ref_piece = jnp.roll(
+        jnp.concatenate(ring[::-1], axis=0), (lax.axis_index("cls") + 1) * ring[0].shape[0], axis=0
+    )
     width_now = ref_piece.shape[0]
     corr = jnp.dot(rotated_rows, ref_piece.T, preferred_element_type=jnp.float32)
     corr = corr.reshape(ROT, n_rows, width_now)

time: 306 us -> 248 us (0.81)
  waiting for transfers between devices: 133 us -> 94.3 us
  local copies, waits for them, and re-layouts: 125 us -> 102 us
  starting transfers between devices: 0.12 us -> 3.29 us
    all_gather x1 -> x0, waiting for transfers between devices: 24.2 us -> none  [on_device(): ref_piece = lax.all_gather(references, 'cls', axis=0, tiled=True)]
    slice x35, local copies, waits for them, and re-layouts: 33.7 us -> 15.8 us  [turned(): return jnp.roll(polar, shift_by, axis=-1).reshape(shape_in)]
    reduce_scatter x1, waiting for transfers between devices: 46.6 us -> 33.7 us  [on_device(): lax.psum_scatter(jnp.einsum('nrk,rnl->kl', weight_cols, rotated, preferre...]
    unnamed x52 -> x61, local copies, waits for them, and re-layouts: 23.6 us -> 17.6 us
    ppermute x0 -> x3, starting transfers between devices: none -> 3.21 us  [on_device(): lax.ppermute(ring[-1], 'cls', [(dev, (dev + 1) % 4) for dev in range(4)])]
  transfers between devices with their start and end apart: 3 -> 5, of which waited for: 3 -> 2; matrix products, arithmetic and copies ran while one was open for 2% -> 53% of each run, Pallas kernels for 0% -> 0%
where the time goes in v1:
time: 248 us; the launch traced here: 243 us
  local copies, waits for them, and re-layouts  102 us (41%)
  waiting for transfers between devices  94.3 us (38%)
  other arithmetic  17.9 us (7%)
  between operations  14.7 us (6%)
  matrix products  11.4 us (5%)
  starting transfers between devices  3.29 us (1%)
    another operation x25, local copies, waits for them, and re-layouts, on_device(): jnp.stack([turned(particles, -r * angle_step) for r in range(ROT)], axis=0)  67.3 us
    reduce_scatter x1, waiting for transfers between devices, on_device(): lax.psum_scatter(local_sums, 'dom', scatter_dimension=1, tiled=True)  60.6 us
    reduce_scatter x1, waiting for transfers between devices, on_device(): lax.psum_scatter(jnp.einsum('nrk,rnl->kl', weight_cols, rotated, preferre...  33.7 us
    unnamed x61, local copies, waits for them, and re-layouts  17.6 us
    slice x35, local copies, waits for them, and re-layouts, turned(): return jnp.roll(polar, shift_by, axis=-1).reshape(shape_in)  15.8 us
    concatenate x23, other arithmetic, turned(): return jnp.roll(polar, shift_by, axis=-1).reshape(shape_in)  15.8 us
    dot_general x1, matrix products, on_device(): jnp.einsum('nrk,rnl->kl', weight_cols, rotated, preferred_element_type=jn...  6.15 us
    dot_general x1, matrix products, on_device(): jnp.dot(rotated_rows, ref_piece.T, preferred_element_type=jnp.float32)  5.2 us
  transfers between devices with their start and end apart: 5, of which 2 were waited for; matrix products, arithmetic and copies ran while one was open for 53% of the time, Pallas kernels for 0%

profile of v1, /device:TPU:0, one launch (start us, length us, event | category | flops | bytes accessed | tf_op | source)
XLA Modules:
  0.0 243.1 jit_solution(11438697066126306425)
XLA Ops:
  32.7 2.6 %collective-permute-start.1 = (bf16[16,16384]{1,0:T(8,128)(2,1)}, bf16[16,16384]{1,0:T(8,128)(2,1)}, u32[]{:S(2)}, u32[]{:S(2)}) collective-permute-start(bf16[16,16384]{1,0:T(8,128)(2,1)} %collective-permute-done), channel_id=1, source_target_pairs={{0,1},{1,2},{2,3},{3,0},{4,5},{5,6},{6,7},{7,4},{8,9},{9,10},{10,1... | collective-permute-start | bytes 1572872 | tf_op jit(solution)/shard_map/ppermute | solution.py:28
  41.2 1.8 stack_reshape.106
  42.9 1.8 stack_reshape.107
  46.4 1.8 stack_reshape.97
  48.2 1.8 stack_reshape.98
  50.0 1.8 stack_reshape.99
  55.3 1.8 stack_reshape.110
  57.1 1.8 stack_reshape.111
  60.6 1.7 stack_reshape.113
  64.2 1.8 stack_reshape.114
  67.8 1.8 stack_reshape.115
  75.0 1.7 stack_reshape.117
  77.8 1.8 stack_reshape.118
  80.8 34.4 %stack.3 = bf16[24,8,16384]{2,0,1:T(8,128)(2,1)} concatenate(bf16[1,8,16384]{2,0,1:T(2,128)(2,1)} %copy.98, bf16[1,8,16384]{2,0,1:T(2,128)(2,1)} %stack_reshape.96, bf16[1,8,16384]{2,0,1:T(2,128)(2,1)} %stack_reshape.97, bf16[1,8,16384]{2,0,1:T(2,128)(2,1)} %stack_reshape.98, bf16[1,8,16384]{2,0,1:T(2,128)(2,1)} %stack_reshape.99, bf16[1,8,16384]{2,0,1:T(2,128)(2,1)S(1)} %stack_reshape.100, ...), dimensions={0} | concatenate | bytes 12582912 | tf_op jit(solution)/shard_map/stack | solution.py:24
  115.2 6.1 %convolution_bitcast_fusion = f32[64,16384]{1,0:T(8,128)} fusion(bf16[24,8,16384]{2,0,1:T(8,128)(2,1)} %stack.3, s32[8,24,64]{2,1,0:T(8,128)S(1)} %copy-done.3, s32[8,64]{1,0:T(8,128)S(1)} %copy-done.2), kind=kOutput, calls=%fused_computation | convolution fusion | flops 402677760 | bytes 10536960 | tf_op jit(solution)/shard_map/nrk,rnl->kl/dot_general | solution.py:39
  121.4 1.9 constant_dynamic-update-slice_fusion.7
  123.4 1.9 constant_dynamic-update-slice_fusion.6
  125.2 1.9 constant_dynamic-update-slice_fusion.5
  127.9 2.0 constant_dynamic-update-slice_fusion.3
  129.9 2.0 constant_dynamic-update-slice_fusion.2
  131.9 1.9 constant_dynamic-update-slice_fusion.1
  133.8 33.7 %reduce-scatter.3.cloned.1.call-done = f32[16,16384]{1,0:T(8,128)} async-done(((f32[64,16384]{1,0:T(8,128)}), f32[16,16384]{1,0:T(8,128)}) %reduce-scatter.3.cloned.1.call-update) | async-done | bytes 1048592 | tf_op jit(solution)/shard_map/reduce_scatter | solution.py:38
  168.4 5.2 %fusion.9 = f32[8,64]{1,0:T(8,128)S(1)} fusion(bf16[24,8,16384]{2,0,1:T(8,128)(2,1)} %stack.3, bf16[128,16384]{1,0:T(8,128)(2,1)} %constant_dynamic-update-slice_fusion, s32[]{:T(128)S(6)} %select_n.14, s32[8,24,64]{2,1,0:T(8,128)S(1)} %copy-done.3, s32[8,64]{1,0:T(8,128)S(1)} %copy-done.2), kind=kOutput, calls=%fused_computation.6 | convolution fusion | flops 402701824 | bytes 8441860 | tf_op jit(solution)/shard_map/dot_general | solution.py:33
  174.2 60.6 %reduce-scatter.5.cloned.1.call-done = f32[16,2048]{1,0:T(8,128)} async-done(((f32[16,16384]{1,0:T(8,128)}), f32[16,2048]{1,0:T(8,128)}) %reduce-scatter.5.cloned.1.call-update) | async-done | bytes 131088 | tf_op jit(solution)/shard_map/reduce_scatter | solution.py:44
  (137 shorter events, 52.9 us)
Async XLA Ops:
  7.2 11.7 %copy-start = (bf16[8,16384]{1,0:T(8,128)(2,1)S(1)}, bf16[8,16384]{1,0:T(8,128)(2,1)}, u32[]{:S(2)}) copy-start(bf16[8,16384]{1,0:T(8,128)(2,1)} %param.4) | copy-start | bytes 786436
  7.2 160.3 %reduce-scatter.3.cloned.1.call-start = ((), (), s32[]{:S(2)}) async-start(), calls=%async_computation.2 | async-start | bytes 5242880 | tf_op jit(solution)/shard_map/reduce_scatter | solution.py:38
  7.2 25.5 %collective-permute-start = (bf16[16,16384]{1,0:T(8,128)(2,1)}, bf16[16,16384]{1,0:T(8,128)(2,1)}, u32[]{:S(2)}, u32[]{:S(2)}) collective-permute-start(bf16[16,16384]{1,0:T(8,128)(2,1)} %param.5), channel_id=1, source_target_pairs={{0,1},{1,2},{2,3},{3,0},{4,5},{5,6},{6,7},{7,4},{8,9},{9,10},{10,1... | collective-permute-start | bytes 1572872 | tf_op jit(solution)/shard_map/ppermute | solution.py:28
  32.7 44.1 %collective-permute-start.1 = (bf16[16,16384]{1,0:T(8,128)(2,1)}, bf16[16,16384]{1,0:T(8,128)(2,1)}, u32[]{:S(2)}, u32[]{:S(2)}) collective-permute-start(bf16[16,16384]{1,0:T(8,128)(2,1)} %collective-permute-done), channel_id=1, source_target_pairs={{0,1},{1,2},{2,3},{3,0},{4,5},{5,6},{6,7},{7,4},{8,9},{9,10},{10,1... | collective-permute-start | bytes 1572872 | tf_op jit(solution)/shard_map/ppermute | solution.py:28
  76.8 44.6 %collective-permute-start.2 = (bf16[16,16384]{1,0:T(8,128)(2,1)}, bf16[16,16384]{1,0:T(8,128)(2,1)}, u32[]{:S(2)}, u32[]{:S(2)}) collective-permute-start(bf16[16,16384]{1,0:T(8,128)(2,1)} %collective-permute-done.1), channel_id=1, source_target_pairs={{0,1},{1,2},{2,3},{3,0},{4,5},{5,6},{6,7},{7,4},{8,9},{9,10},{10,1... | collective-permute-start | bytes 1572872 | tf_op jit(solution)/shard_map/ppermute | solution.py:28
  80.8 34.4 %copy-start.2 = (s32[8,64]{1,0:T(8,128)S(1)}, s32[8,64]{1,0:T(8,128)}, u32[]{:S(2)}) copy-start(s32[8,64]{1,0:T(8,128)} %param.7) | copy-start | bytes 6148
  80.8 34.4 %copy-start.3 = (s32[8,24,64]{2,1,0:T(8,128)S(1)}, s32[8,24,64]{2,1,0:T(8,128)}, u32[]{:S(2)}) copy-start(s32[8,24,64]{2,1,0:T(8,128)} %param.6) | copy-start | bytes 147460
  121.3 5.8 %copy-start.1 = (bf16[16,16384]{1,0:T(8,128)(2,1)S(1)}, bf16[16,16384]{1,0:T(8,128)(2,1)}, u32[]{:S(2)}) copy-start(bf16[16,16384]{1,0:T(8,128)(2,1)} %param.5) | copy-start | bytes 1572868
  121.3 113.4 %reduce-scatter.5.cloned.1.call-start = ((), (), s32[]{:S(2)}) async-start(), calls=%async_computation.3 | async-start | bytes 1179648 | tf_op jit(solution)/shard_map/reduce_scatter | solution.py:44
Sparse Core Ops, SparseCore 0:
  121.5 46.0 reduce-scatter.2
  171.3 63.3 reduce-scatter.4
